TPU v7x, 512 devices: a whole 4x4x16 slice. The times are simulated.
512 devices in a mesh: pair: 64 (over x, z), ri: 8 (over y, core).
Axes of the slice: x: 4, y: 4, z: 16, core: 2. Of those that a mesh axis runs over, the one named last changes fastest.
Arguments:
- tensor: bfloat16 [64, 2048, 2304], P('pair', 'ri'), may hold values from -0.5 to 0.5
- pattern: int32 [64, 64], P('pair', 'ri'), may hold values 0 or 1
- pair_blocks: int32 [64, 2], replicated, may hold values from 0 to 11, as said below
- green_occ: bfloat16 [576, 576], replicated, may hold values from -0.25 to 0.25
- green_virt: bfloat16 [576, 576], replicated, may hold values from -0.25 to 0.25
Outputs:
- chi: float32 [2048, 2048], P('ri', 'pair')
Inputs may be any that keep to these rules, and one draw needn't show every extreme that they name: `pair_blocks`: no pair of blocks appears twice.
All inputs are finite; a program needn't handle non-finite values. No bound on the sum of `pattern` on one device may be relied on, other than what follows from the above.
Results may differ from a plain program's by a relative error of at most 0.0041.
Values may be sent and summed in bfloat16 or wider, within the bound.
A program may use at most 64 MiB of HBM per device.

v0:
```python
import jax
import jax.numpy as jnp
from jax import lax
from jax.sharding import PartitionSpec as P

BLK = 48
NB = 12
RB = 32
BB = 2304


def build_images(blocks, index, green_occ, green_virt):
    count = blocks.shape[0]
    dense = jnp.zeros((count, NB * NB, BB), blocks.dtype).at[:, index].set(blocks)
    dense = (
        dense.reshape(count, NB, NB, BLK, BLK)
        .transpose(0, 1, 3, 2, 4)
        .reshape(count, NB * BLK, NB * BLK)
    )
    half = jnp.einsum("qms,ts->qmt", dense, green_virt, preferred_element_type=jnp.float32).astype(
        jnp.bfloat16
    )
    full = jnp.einsum("lm,qmt->qlt", green_occ, half, preferred_element_type=jnp.float32).astype(
        jnp.bfloat16
    )
    full = (
        full.reshape(count, NB, BLK, NB, BLK).transpose(0, 1, 3, 2, 4).reshape(count, NB * NB, BB)
    )
    return full[:, index]


def on_device(tensor, pattern, pair_blocks, green_occ, green_virt):
    pairs_here = tensor.shape[0]
    ri_here = tensor.shape[1]
    width = tensor.shape[2]
    groups = lax.axis_size("pair")
    per_group = ri_here // groups
    mask = jnp.repeat(pattern, RB, axis=1).astype(tensor.dtype)
    masked = tensor * mask[:, :, None]
    index = pair_blocks[:, 0] * NB + pair_blocks[:, 1]
    sending = masked.reshape(pairs_here, groups, per_group, width)
    blocks = lax.all_to_all(sending, "pair", split_axis=1, concat_axis=0, tiled=True)[
        :, 0
    ].transpose(1, 0, 2)
    made = build_images(blocks, index, green_occ, green_virt)
    exchanged = made.transpose(1, 0, 2)[:, None]
    returned = lax.all_to_all(exchanged, "pair", split_axis=0, concat_axis=1, tiled=True)
    images = returned.reshape(pairs_here, ri_here, width)
    gathered = lax.all_gather(images, "ri", axis=1, tiled=True)
    partial_chi = jnp.einsum("pak,pbk->ab", masked, gathered, preferred_element_type=jnp.float32)
    return lax.psum_scatter(partial_chi, "pair", scatter_dimension=1, tiled=True)


def solution(mesh):
    in_specs = (P("pair", "ri", None), P("pair", "ri"), P(), P(), P())
    out_specs = P("ri", "pair")
    return jax.shard_map(
        on_device, mesh=mesh, in_specs=in_specs, out_specs=out_specs, check_vma=False
    )
```

profile of v0, /device:TPU:7, one launch (start us, length us, event | category | flops | bytes accessed | tf_op | source)
XLA Modules:
  0.0 982.9 jit_solution(9961822255055989414)
XLA Ops:
  6.5 0.0 copy-start
  6.5 0.7 convert_bitcast_fusion.1
  7.3 0.1 broadcast_in_dim.12
  7.3 0.1 convert_element_type.27
  7.4 1.4 broadcast_multiply_fusion
  8.9 0.0 copy-start.2
  8.9 0.0 copy-start.6
  8.9 1.4 reshape.50
  10.3 18.2 %all-to-all-start = ((bf16[1,64,4,2304]{3,2,0,1:T(4,128)(2,1)}), bf16[1,64,4,2304]{3,2,0,1:T(4,128)(2,1)S(1)}, u32[]{:S(2)}, u32[]{:S(2)}) async-start(bf16[1,64,4,2304]{3,2,0,1:T(4,128)(2,1)} %reshape.50), calls=%async_computation | async-start | bytes 2359296 | tf_op jit(solution)/shard_map/all_to_all | solution.py:42
  28.5 0.0 all-gather.2.cloned.1.call-start
  28.6 0.0 copy-done.6
  28.6 55.6 %all-to-all-done = bf16[1,64,4,2304]{3,2,0,1:T(4,128)(2,1)S(1)} async-done(((bf16[1,64,4,2304]{3,2,0,1:T(4,128)(2,1)}), bf16[1,64,4,2304]{3,2,0,1:T(4,128)(2,1)S(1)}, u32[]{:S(2)}, u32[]{:S(2)}) %all-to-all-start) | async-done | bytes 1179680 | tf_op jit(solution)/shard_map/all_to_all | solution.py:42
  84.2 0.0 copy-done.2
  84.2 0.0 copy-start.4
  84.2 1.0 copy-done.4
  85.2 0.7 broadcast_in_dim.13
  85.9 6.3 scatter_fusion
  92.2 8.3 reshape.51
  100.5 13.9 %copy.20 = bf16[4,12,12,48,48]{4,2,3,1,0:T(8,128)(2,1)} copy(bf16[4,12,12,48,48]{4,3,0,2,1:T(8,128)(2,1)} %reshape.51) | data formatting | bytes 5308416 | tf_op jit(solution)/shard_map/reshape | solution.py:16
  114.4 0.0 copy-start.5
  114.4 12.6 %reshape.52 = bf16[4,576,576]{2,1,0:T(8,128)(2,1)} reshape(bf16[4,12,48,12,48]{4,3,2,1,0:T(8,128)(2,1)} %bitcast.34) | data formatting | bytes 5308416 | tf_op jit(solution)/shard_map/reshape | solution.py:18
  127.1 0.0 copy-done
  127.1 0.0 copy-done.5
  127.1 8.8 convert_bitcast_fusion
  135.9 4.6 copy.12
  140.5 13.8 %reshape.53 = bf16[4,12,48,12,48]{4,3,2,1,0:T(8,128)(2,1)} reshape(bf16[4,576,576]{2,1,0:T(8,128)(2,1)} %copy.12) | data formatting | bytes 5308416 | tf_op jit(solution)/shard_map/reshape | solution.py:27
  154.3 8.3 copy.17
  162.6 9.9 %reshape.75 = bf16[4,144,2304]{2,0,1:T(4,128)(2,1)S(1)} reshape(bf16[4,12,12,48,48]{4,3,0,2,1:T(8,128)(2,1)} %copy.17) | data formatting | bytes 5308416 | tf_op jit(solution)/shard_map/reshape | solution.py:27
  172.5 2.5 gather_fusion
  175.0 0.0 copy-start.3
  175.0 66.3 %all_to_all.8 = bf16[64,1,4,2304]{3,2,1,0:T(4,128)(2,1)S(1)} all-to-all(bf16[64,1,4,2304]{3,2,1,0:T(4,128)(2,1)} %bitcast.36), channel_id=1, replica_groups=mesh['pair'=64,'ri'=8] {'pair'}, dimensions={0} | all-to-all | bytes 2359296 | tf_op jit(solution)/shard_map/all_to_all | solution.py:47
  241.3 1.2 reshape.55
  242.5 0.0 all-gather.2.cloned.1.call-update
  242.5 0.0 reduce-scatter.2.cloned.1.call-start
  242.5 59.2 %all-gather.2.cloned.1.call-done = bf16[1,2048,2304]{2,1,0:T(8,128)(2,1)} async-done(((bf16[1,256,2304]{2,1,0:T(8,128)(2,1)}), bf16[1,2048,2304]{2,1,0:T(8,128)(2,1)}) %all-gather.2.cloned.1.call-update) | async-done | bytes 9437200 | tf_op jit(solution)/shard_map/all_gather | solution.py:49
  301.7 0.0 copy-done.3
  301.7 0.0 copy-start.1
  301.7 7.7 fusion
  309.4 0.0 reduce-scatter.2.cloned.1.call-update
  309.5 666.6 %reduce-scatter.2.cloned.1.call-done = f32[256,32]{0,1:T(8,128)} async-done(((f32[256,2048]{0,1:T(8,128)}), f32[256,32]{0,1:T(8,128)}) %reduce-scatter.2.cloned.1.call-update) | async-done | bytes 32784 | tf_op jit(solution)/shard_map/reduce_scatter | solution.py:51
  976.1 0.0 copy-done.1
  (2 shorter events, 0.0 us)
Async XLA Ops:
  6.5 120.5 %copy-start = (bf16[576,576]{1,0:T(8,128)(2,1)S(1)}, bf16[576,576]{1,0:T(8,128)(2,1)}, u32[]{:S(2)}) copy-start(bf16[576,576]{1,0:T(8,128)(2,1)} %param.8) | copy-start | bytes 1990660
  8.9 75.3 %copy-start.2 = (bf16[1,256,2304]{2,1,0:T(8,128)(2,1)}, bf16[1,256,2304]{2,1,0:T(8,128)(2,1)S(1)}, u32[]{:S(2)}) copy-start(bf16[1,256,2304]{2,1,0:T(8,128)(2,1)S(1)} %broadcast_multiply_fusion) | copy-start | bytes 3538948
  8.9 19.7 %copy-start.6 = (s32[64,2]{0,1:T(2,128)S(1)}, s32[64,2]{0,1:T(2,128)}, u32[]{:S(2)}) copy-start(s32[64,2]{0,1:T(2,128)} %param.7) | copy-start | bytes 1540
  10.3 73.9 %all-to-all-start = ((bf16[1,64,4,2304]{3,2,0,1:T(4,128)(2,1)}), bf16[1,64,4,2304]{3,2,0,1:T(4,128)(2,1)S(1)}, u32[]{:S(2)}, u32[]{:S(2)}) async-start(bf16[1,64,4,2304]{3,2,0,1:T(4,128)(2,1)} %reshape.50), calls=%async_computation | async-start | bytes 2359296 | tf_op jit(solution)/shard_map/all_to_all | solution.py:42
  28.5 273.2 %all-gather.2.cloned.1.call-start = ((), (), s32[]{:S(2)}) async-start(), calls=%async_computation.3 | async-start | bytes 10616832 | tf_op jit(solution)/shard_map/all_gather | solution.py:49
  84.2 1.0 copy-start.4
  114.4 12.6 %copy-start.5 = (bf16[576,576]{1,0:T(8,128)(2,1)S(1)}, bf16[576,576]{1,0:T(8,128)(2,1)}, u32[]{:S(2)}) copy-start(bf16[576,576]{1,0:T(8,128)(2,1)} %param.9) | copy-start | bytes 1990660
  175.0 126.7 %copy-start.3 = (bf16[1,256,2304]{2,1,0:T(8,128)(2,1)S(1)}, bf16[1,256,2304]{2,1,0:T(8,128)(2,1)}, u32[]{:S(2)}) copy-start(bf16[1,256,2304]{2,1,0:T(8,128)(2,1)} %copy-done.2) | copy-start | bytes 3538948
  242.5 733.6 %reduce-scatter.2.cloned.1.call-start = ((), (), s32[]{:S(2)}) async-start(), calls=%async_computation.4 | async-start | bytes 2129920 | tf_op jit(solution)/shard_map/reduce_scatter | solution.py:51
  301.7 674.4 %copy-start.1 = (bf16[576,576]{1,0:T(8,128)(2,1)S(1)}, bf16[576,576]{1,0:T(8,128)(2,1)}, u32[]{:S(2)}) copy-start(bf16[576,576]{1,0:T(8,128)(2,1)} %param.8) | copy-start | bytes 1990660
Sparse Core Ops, SparseCore 0:
  242.6 59.0 all-gather.1
  309.6 666.4 reduce-scatter.1
where the time goes:
time: 996 us; the launch traced here: 983 us
  waiting for transfers between devices  781 us (78%)
  local copies, waits for them, and re-layouts  84.7 us (9%)
  blocking collectives  66.3 us (7%)
  starting transfers between devices  18.3 us (2%)
  matrix products  16.6 us (2%)
  between operations  13.5 us (1%)
    reduce_scatter x1, waiting for transfers between devices, on_device(): lax.psum_scatter(partial_chi, 'pair', scatter_dimension=1, tiled=True)  667 us
    all_to_all x1, blocking collectives, on_device(): lax.all_to_all(exchanged, 'pair', split_axis=0, concat_axis=1, tiled=True)  66.3 us
    all_gather x1, waiting for transfers between devices, on_device(): gathered = lax.all_gather(images, 'ri', axis=1, tiled=True)  59.2 us
    all_to_all x1, waiting for transfers between devices, on_device(): lax.all_to_all(sending, 'pair', split_axis=1, concat_axis=0, tiled=True)  55.6 us
    reshape x3, local copies, waits for them, and re-layouts, build_images(): full.reshape(count, NB, BLK, NB, BLK).transpose(0, 1, 3, 2, 4)  32 us
    reshape x2, local copies, waits for them, and re-layouts, build_images(): dense.reshape(count, NB, NB, BLK, BLK).transpose(0, 1, 3, 2, 4)  22.2 us
  transfers between devices with their start and end apart: 3, of which 3 were waited for; matrix products, arithmetic and copies ran while one was open for 0% of the time, Pallas kernels for 0%

commit v1 on v0

v1 whole, which is shorter than its diff:
```python
import jax
import jax.numpy as jnp
from jax import lax
from jax.experimental import pallas as pl
from jax.experimental.pallas import tpu as pltpu
from jax.sharding import PartitionSpec as P

BLK = 48
NB = 12
RB = 32
BB = 2304
NX, NY, NZ = 4, 4, 16
GROUPS = NX * NZ
MESH = pl.DeviceIdType.MESH
BF = jnp.bfloat16
F32 = jnp.float32


def nt(a, b):
    return lax.dot_general(a, b, (((1,), (1,)), ((), ())), preferred_element_type=F32)


def nn(a, b):
    return jnp.dot(a, b, preferred_element_type=F32)


def one_hot(rows, cols, match):
    r = lax.broadcasted_iota(jnp.int32, (rows, cols), 0)
    c = lax.broadcasted_iota(jnp.int32, (rows, cols), 1)
    return jnp.where(match(r, c), 1.0, 0.0).astype(BF)


def pad64(r, u):
    return (u == BLK * lax.div(r, 64) + lax.rem(r, 64)) & (lax.rem(r, 64) < BLK)


def pad80(r, u):
    return (u == 8 * lax.rem(r, 80) + lax.div(r, 80)) & (lax.rem(r, 80) < 72)


def by_q(r, c):
    q, w = lax.div(r, 80), lax.rem(r, 80)
    return (c == lax.div(w, 6) * 32 + q * 6 + lax.rem(w, 6)) & (w < 72)


def by_block(r, c):
    return by_q(c, r)


def by_m(r, c):
    mh, rest = lax.div(r, 32), lax.rem(r, 32)
    return c == rest * 6 + mh


def kernel(
    inv, pb, send1, dm, gv, go, out,
    recv1, dall, dense, xs, ys, ws, send2, recv2, img, xsend, xrecv, zsend, zrecv, fsend,
    gvp, gop, pa, pbk, pc,
    s1, r1, sy, ry, s2, r2, sx, rx, sz, rz, sf, rf, local,
):
    me = lax.axis_index("pair")
    ri = lax.axis_index("ri")
    x, z = lax.div(me, NZ), lax.rem(me, NZ)
    y, core = lax.div(ri, 2), lax.rem(ri, 2)
    sib = y * 2 + 1 - core
    up = lax.rem(y + 1, NY) * 2 + core
    down = lax.rem(y + NY - 1, NY) * 2 + core
    far = lax.rem(y + 2, NY) * 2 + core

    bar = pltpu.get_barrier_semaphore()

    def greet(pair, r):
        pl.semaphore_signal(bar, inc=1, device_id={"pair": pair, "ri": r}, device_id_type=MESH)

    def greet_pair(k, c):
        greet(lax.rem(me + k, GROUPS), ri)
        return c

    lax.fori_loop(1, GROUPS, greet_pair, 0)
    for k in range(NZ):
        greet(x * NZ + lax.rem(z + k, NZ), sib)
    greet(me, up)
    greet(me, down)

    @pl.when(x != y)
    def _():
        greet(y * NZ + z, x * 2 + core)

    pl.semaphore_wait(bar, GROUPS - 1 + NZ + 2 + jnp.where(x != y, 1, 0))

    def swap(src, dst, ss, rs, k):
        to = lax.rem(me + k, GROUPS)
        return pltpu.make_async_remote_copy(
            src_ref=src.at[to], dst_ref=dst.at[me], send_sem=ss.at[k], recv_sem=rs.at[me],
            device_id={"pair": to}, device_id_type=MESH,
        )

    def swapped(src, dst, ss, rs, k):
        fro = lax.rem(me + k, GROUPS)
        return pltpu.make_async_remote_copy(
            src_ref=src.at[fro], dst_ref=dst.at[fro], send_sem=ss.at[k], recv_sem=rs.at[fro],
            device_id={"pair": fro}, device_id_type=MESH,
        )

    def along(src, dst, i, to):
        return pltpu.make_async_remote_copy(
            src_ref=src, dst_ref=dst, send_sem=sy.at[i], recv_sem=ry.at[i],
            device_id={"ri": to}, device_id_type=MESH,
        )

    def start1(k, c):
        swap(send1, recv1, s1, r1, k).start()
        return c

    g_up = along(dm, dall.at[ri], 0, up)
    g_down = along(dm, dall.at[ri], 1, down)
    g_sib = along(dm, dall.at[ri], 2, sib)
    g_up.start()
    g_down.start()
    lax.fori_loop(1, GROUPS, start1, 0)
    g_sib.start()
    own1 = pltpu.make_async_copy(send1.at[me], recv1.at[me], local.at[0])
    own1.start()
    ownd = pltpu.make_async_copy(dm, dall.at[ri], local.at[1])
    ownd.start()
    recv1[GROUPS] = jnp.zeros((24, 384), BF)

    e = one_hot(768, 576, pad64)
    gvp[...] = nt(nt(e, gv[...]).astype(BF), e).astype(BF)
    f = one_hot(640, 576, pad80)
    gop[...] = nt(nn(f, go[...]).astype(BF), f).astype(BF)
    pa[...] = one_hot(320, 384, by_q)
    pbk[...] = one_hot(384, 320, by_block)
    pc[...] = one_hot(192, 192, by_m)

    half = pl.ds(0, 128)
    rest = pl.ds(128, 128)
    along(dm, dall.at[down], 0, up).wait_recv()
    h_up = along(dall.at[down, half], dall.at[down, half], 3, up)
    h_up.start()
    f_down = along(dall.at[down], dall.at[down], 4, sib)
    f_down.start()
    along(dm, dall.at[up], 1, down).wait_recv()
    h_down = along(dall.at[up, rest], dall.at[up, rest], 5, down)
    h_down.start()
    f_up = along(dall.at[up], dall.at[up], 6, sib)
    f_up.start()

    own1.wait()

    def end1(k, c):
        swapped(send1, recv1, s1, r1, k).wait()
        return c

    lax.fori_loop(1, GROUPS, end1, 0)

    def place(n, c):
        i, jp = lax.div(n, 6), lax.rem(n, 6)
        lowr = jnp.zeros((8, 384), BF)
        b0 = jnp.concatenate([recv1[inv[2 * n]], lowr], axis=0)
        b1 = jnp.concatenate([recv1[inv[2 * n + 1]], lowr], axis=0)
        gap = jnp.zeros((32, 16), BF)
        low = jnp.zeros((8, 128), BF)
        for a in range(8):
            cut = slice(a * BLK, (a + 1) * BLK)
            row = jnp.concatenate([b0[:, cut], gap, b1[:, cut], gap], axis=1)
            dense[a, jp, i] = row
        return c

    lax.fori_loop(0, 72, place, 0)

    def first(a, c):
        d = jnp.concatenate([dense[a, jp].reshape(384, 128) for jp in range(6)], axis=1)
        d = nn(pa[...], d).astype(BF)
        h = nn(d, gvp[...]).astype(BF)
        for q in range(4):
            xs[q, a] = h[q * 80 : (q + 1) * 80]
        return c

    lax.fori_loop(0, 8, first, 0)

    def second(q, c):
        v = nn(gop[...], xs[q].reshape(640, 768)).astype(BF)
        for a in range(8):
            ys[a, q] = v[a * 80 : (a + 1) * 80]
        return c

    lax.fori_loop(0, 4, second, 0)

    def third(a, c):
        v = nn(pbk[...], ys[a].reshape(320, 768)).astype(BF)
        for tp in range(6):
            ws[a, tp] = v[:, tp * 128 : (tp + 1) * 128].reshape(12, 32, 128)
        return c

    lax.fori_loop(0, 8, third, 0)

    def pack(p):
        l, t = pb[2 * p], pb[2 * p + 1]
        tp, odd = lax.div(t, 2), lax.rem(t, 2)
        cols = []
        for a in range(8):
            w = ws[a, tp, l]
            cols.append(jnp.where(odd == 1, w[:24, 64:112], w[:24, 0:48]))
        send2[p] = jnp.concatenate(cols, axis=1)

    def start2(k, c):
        pack(lax.rem(me + k, GROUPS))
        swap(send2, recv2, s2, r2, k).start()
        return c

    lax.fori_loop(1, GROUPS, start2, 0)
    pack(me)
    own2 = pltpu.make_async_copy(send2.at[me], recv2.at[me], local.at[2])
    own2.start()

    along(dm.at[half], dall.at[far, half], 3, up).wait_recv()
    along(dm.at[rest], dall.at[far, rest], 5, down).wait_recv()
    f_far = along(dall.at[far], dall.at[far], 7, sib)
    f_far.start()
    ownd.wait()
    g_sib.wait_recv()
    f_down.wait_recv()
    f_up.wait_recv()
    f_far.wait_recv()
    own2.wait()

    def end2(k, c):
        swapped(send2, recv2, s2, r2, k).wait()
        return c

    lax.fori_loop(1, GROUPS, end2, 0)

    for g in range(8):
        v = nn(pc[...], recv2[g * 8 : (g + 1) * 8].reshape(192, 384)).astype(BF)
        for mh in range(6):
            img[g * 32 : (g + 1) * 32, mh * 384 : (mh + 1) * 384] = v[mh * 32 : (mh + 1) * 32]

    def part(xt):
        return jnp.concatenate([nt(img[...], dall[2 * xt]), nt(img[...], dall[2 * xt + 1])], axis=1)

    def across(k):
        return pltpu.make_async_remote_copy(
            src_ref=xsend.at[k], dst_ref=xrecv.at[k], send_sem=sx.at[k], recv_sem=rx.at[k],
            device_id={"pair": lax.rem(x + k + 1, NX) * NZ + z}, device_id_type=MESH,
        )

    for k in (1, 0, 2):
        xsend[k] = part(lax.rem(x + k + 1, NX)).astype(BF)
        across(k).start()
    total = part(x)
    for k in (1, 0, 2):
        across(k).wait()
        total = total + xrecv[k].astype(F32)
    total = total.astype(BF)
    for h in range(2):
        for q in range(8):
            zsend[q, h] = total[q * 32 : (q + 1) * 32, h * 256 : (h + 1) * 256]

    def deal(q, h):
        return pltpu.make_async_remote_copy(
            src_ref=zsend.at[q, h], dst_ref=zrecv.at[z], send_sem=sz.at[q, h], recv_sem=rz.at[z],
            device_id={"pair": x * NZ + core * 8 + q, "ri": y * 2 + h}, device_id_type=MESH,
        )

    def dealt(fro):
        return pltpu.make_async_remote_copy(
            src_ref=zsend.at[0, 0], dst_ref=zrecv.at[fro], send_sem=sz.at[0, 0],
            recv_sem=rz.at[fro], device_id={"pair": x * NZ + fro, "ri": ri}, device_id_type=MESH,
        )

    mine = lax.div(z, 8) == core
    zq = lax.rem(z, 8)
    for step in range(8):
        q = lax.rem(zq + step, 8)
        for h in range(2):
            if step == 0:
                same = mine & (core == h)

                @pl.when(same)
                def _():
                    pltpu.make_async_copy(zsend.at[q, h], zrecv.at[z], local.at[3]).start()

                @pl.when(jnp.logical_not(same))
                def _():
                    deal(q, h).start()
            else:
                deal(q, h).start()
    for step in range(8):
        q = lax.rem(zq + step, 8)
        for h in range(2):
            if step == 0:
                same = mine & (core == h)

                @pl.when(jnp.logical_not(same))
                def _():
                    deal(q, h).wait_send()
            else:
                deal(q, h).wait_send()

    @pl.when(mine)
    def _():
        pltpu.make_async_copy(zsend.at[0, 0], zrecv.at[z], local.at[3]).wait()

    @pl.when(jnp.logical_not(mine))
    def _():
        dealt(z).wait_recv()

    def end3(k, c):
        dealt(lax.rem(z + k, NZ)).wait_recv()
        return c

    lax.fori_loop(1, NZ, end3, 0)
    result = zrecv[0].astype(F32)
    for k in range(1, NZ):
        result = result + zrecv[k].astype(F32)

    @pl.when(x == y)
    def _():
        out[...] = result

    @pl.when(x != y)
    def _():
        fsend[...] = result
        turn = pltpu.make_async_remote_copy(
            src_ref=fsend, dst_ref=out, send_sem=sf, recv_sem=rf,
            device_id={"pair": y * NZ + z, "ri": x * 2 + core}, device_id_type=MESH,
        )
        turn.start()
        turn.wait()

    g_up.wait_send()
    g_down.wait_send()
    g_sib.wait_send()
    h_up.wait_send()
    h_down.wait_send()
    f_down.wait_send()
    f_up.wait_send()
    f_far.wait_send()


def on_device(tensor, pattern, pair_blocks, green_occ, green_virt):
    mask = jnp.repeat(pattern, RB, axis=1).astype(tensor.dtype)
    masked = (tensor * mask[:, :, None])[0]
    index = pair_blocks[:, 0] * NB + pair_blocks[:, 1]
    hits = index[None, :] == jnp.arange(NB * NB, dtype=jnp.int32)[:, None]
    order = jnp.arange(GROUPS, dtype=jnp.int32)[None, :]
    inverse = jnp.min(jnp.where(hits, order, GROUPS), axis=1).astype(jnp.int32)
    vmem = pl.BlockSpec(memory_space=pltpu.VMEM)
    smem = pl.BlockSpec(memory_space=pltpu.SMEM)
    dma = pltpu.SemaphoreType.DMA
    chi = pl.pallas_call(
        kernel,
        out_shape=jax.ShapeDtypeStruct((32, 256), F32),
        in_specs=[smem, smem, vmem, vmem, vmem, vmem],
        out_specs=vmem,
        scratch_shapes=[
            pltpu.VMEM((GROUPS + 1, 24, 384), BF),
            pltpu.VMEM((8, 256, BB), BF),
            pltpu.VMEM((8, 6, 12, 32, 128), BF),
            pltpu.VMEM((4, 8, 80, 768), BF),
            pltpu.VMEM((8, 4, 80, 768), BF),
            pltpu.VMEM((8, 6, 12, 32, 128), BF),
            pltpu.VMEM((GROUPS, 24, 384), BF),
            pltpu.VMEM((GROUPS, 24, 384), BF),
            pltpu.VMEM((256, BB), BF),
            pltpu.VMEM((3, 256, 512), BF),
            pltpu.VMEM((3, 256, 512), BF),
            pltpu.VMEM((8, 2, 32, 256), BF),
            pltpu.VMEM((NZ, 32, 256), BF),
            pltpu.VMEM((32, 256), F32),
            pltpu.VMEM((768, 768), BF),
            pltpu.VMEM((640, 640), BF),
            pltpu.VMEM((320, 384), BF),
            pltpu.VMEM((384, 320), BF),
            pltpu.VMEM((192, 192), BF),
            dma((GROUPS,)), dma((GROUPS,)),
            dma((8,)), dma((8,)),
            dma((GROUPS,)), dma((GROUPS,)),
            dma((3,)), dma((3,)),
            dma((8, 2)), dma((NZ,)),
            dma, dma,
            dma((4,)),
        ],
        compiler_params=pltpu.CompilerParams(
            collective_id=0, has_side_effects=True, vmem_limit_bytes=60 << 20
        ),
    )(inverse, pair_blocks.reshape(-1), masked.reshape(GROUPS, 24, 384), masked, green_virt, green_occ)
    return chi.T


def solution(mesh):
    in_specs = (P("pair", "ri", None), P("pair", "ri"), P(), P(), P())
    out_specs = P("ri", "pair")
    return jax.shard_map(
        on_device, mesh=mesh, in_specs=in_specs, out_specs=out_specs, check_vma=False
    )
```

time: 996 us -> 194 us (0.19); the launches traced: 983 us -> 193 us
  waiting for transfers between devices: 781 us -> 0 us
  Pallas kernels: 0 us -> 184 us
  local copies, waits for them, and re-layouts: 84.7 us -> 4.21 us
  blocking collectives: 66.3 us -> 0 us
  starting transfers between devices: 18.3 us -> 0 us
  matrix products: 16.6 us -> 0 us
  between operations: 13.5 us -> 0.03 us
    reduce_scatter x1 -> x0, waiting for transfers between devices: 667 us -> none  [on_device(): lax.psum_scatter(partial_chi, 'pair', scatter_dimension=1, tiled=True)]
    pallas_call x0 -> x1, Pallas kernels: none -> 184 us  [on_device(): pl.pallas_call(kernel, out_shape=jax.ShapeDtypeStruct((32, 256), F32), in...]
    reshape x8 -> x1, local copies, waits for them, and re-layouts: 69.4 us -> 0.73 us  [on_device(): pair_blocks.reshape(-1)]
    all_to_all x1 -> x0, blocking collectives: 66.3 us -> none  [on_device(): lax.all_to_all(exchanged, 'pair', split_axis=0, concat_axis=1, tiled=True)]
    all_gather x1 -> x0, waiting for transfers between devices: 59.2 us -> none  [on_device(): gathered = lax.all_gather(images, 'ri', axis=1, tiled=True)]
    all_to_all x1 -> x0, waiting for transfers between devices: 55.6 us -> none  [on_device(): lax.all_to_all(sending, 'pair', split_axis=1, concat_axis=0, tiled=True)]
    all_to_all x1 -> x0, starting transfers between devices: 18.2 us -> none  [on_device(): lax.all_to_all(sending, 'pair', split_axis=1, concat_axis=0, tiled=True)]
    dot_general x2 -> x0, matrix products: 16.6 us -> none  [the longest x1 8.85 us: build_images(): jnp.einsum('lm,qmt->qlt', green_occ, half, preferred_element_type=jnp.flo...]
  transfers between devices with their start and end apart: 3 -> 0, of which waited for: 3 -> 0; matrix products, arithmetic and copies ran while one was open for 0% -> 0% of each run, Pallas kernels for 0% -> 0%
where the time goes in v1:
time: 194 us; the launch traced here: 193 us
  Pallas kernels  184 us (95%)
  local copies, waits for them, and re-layouts  4.21 us (2%)
  other arithmetic  3.93 us (2%)
    pallas_call x1, Pallas kernels, on_device(): pl.pallas_call(kernel, out_shape=jax.ShapeDtypeStruct((32, 256), F32), in...  184 us

profile of v1, /device:TPU:7, one launch (start us, length us, event | category | flops | bytes accessed | tf_op | source)
XLA Modules:
  0.0 192.5 jit_solution(5387481290038730985)
XLA Ops:
  0.0 0.7 convert_bitcast_fusion
  0.7 0.1 broadcast_in_dim.21
  0.7 0.1 convert_element_type.18
  0.8 1.4 broadcast_multiply_fusion
  2.2 0.0 copy-start
  2.3 1.8 reshape_squeeze.3.send1
  4.1 0.0 copy-done
  4.1 0.0 copy-start.1
  4.1 1.2 fusion.dm
  5.3 0.0 copy-done.1
  5.3 0.1 copy.8
  5.4 0.7 reshape.33.pb
  6.1 0.7 select_reduce_fusion.inv
  6.8 184.3 %shard_map.55 = f32[32,256]{1,0:T(8,128)} custom-call(s32[144]{0:T(256)} %select_reduce_fusion.inv, s32[128]{0:T(128)} %reshape.33.pb, bf16[64,24,384]{2,1,0:T(8,128)(2,1)} %reshape_squeeze.3.send1, bf16[256,2304]{1,0:T(8,128)(2,1)} %fusion.dm, bf16[576,576]{1,0:T(8,128)(2,1)} %gv.1, bf16[576,576]{1,0:T(8,128)(2,1)} %go.1), custom_call_target="tpu_custom_call" | custom-call | tf_op jit(solution)/shard_map/pallas_call | solution.py:352
  191.2 1.4 copy.10
  (1 shorter events, 0.0 us)
Async XLA Ops:
  2.2 1.9 copy-start
  4.1 1.2 copy-start.1

commit v2 on v1

--- a/solution.py
+++ b/solution.py
@@ -11,6 +11,10 @@
 BB = 2304
 NX, NY, NZ = 4, 4, 16
 GROUPS = NX * NZ
+TURNS = 2
+SHARE = GROUPS // TURNS
+ZT = NZ // TURNS
+ZROWS = 32 // TURNS
 MESH = pl.DeviceIdType.MESH
 BF = jnp.bfloat16
 F32 = jnp.float32
@@ -47,14 +51,18 @@
     return by_q(c, r)
 
 
+def from_m(r, c):
+    return by_m(c, r)
+
+
 def by_m(r, c):
     mh, rest = lax.div(r, 32), lax.rem(r, 32)
     return c == rest * 6 + mh
 
 
 def kernel(
-    inv, pb, send1, dm, gv, go, out,
-    recv1, dall, dense, xs, ys, ws, send2, recv2, img, xsend, xrecv, zsend, zrecv, fsend,
+    inv, pb, pattern, tensor, gv, go, out,
+    send1, dm, recv1, dall, dense, xs, ys, ws, send2, recv2, img, xsend, xrecv, zsend, zrecv, fsend,
     gvp, gop, pa, pbk, pc,
     s1, r1, sy, ry, s2, r2, sx, rx, sz, rz, sf, rf, local,
 ):
@@ -86,21 +94,15 @@
     def _():
         greet(y * NZ + z, x * 2 + core)
 
+    pc[...] = one_hot(192, 192, from_m)
+    for g in range(8):
+        rows = slice(g * RB, (g + 1) * RB)
+        masked = tensor[0, rows] * pattern[0, g].astype(BF)
+        dm[rows] = masked
+        v = jnp.concatenate([masked[:, m * 384 : (m + 1) * 384] for m in range(6)], axis=0)
+        send1[g * 8 : (g + 1) * 8] = nn(pc[...], v).astype(BF).reshape(8, 24, 384)
+
     pl.semaphore_wait(bar, GROUPS - 1 + NZ + 2 + jnp.where(x != y, 1, 0))
-
-    def swap(src, dst, ss, rs, k):
-        to = lax.rem(me + k, GROUPS)
-        return pltpu.make_async_remote_copy(
-            src_ref=src.at[to], dst_ref=dst.at[me], send_sem=ss.at[k], recv_sem=rs.at[me],
-            device_id={"pair": to}, device_id_type=MESH,
-        )
-
-    def swapped(src, dst, ss, rs, k):
-        fro = lax.rem(me + k, GROUPS)
-        return pltpu.make_async_remote_copy(
-            src_ref=src.at[fro], dst_ref=dst.at[fro], send_sem=ss.at[k], recv_sem=rs.at[fro],
-            device_id={"pair": fro}, device_id_type=MESH,
-        )
 
     def along(src, dst, i, to):
         return pltpu.make_async_remote_copy(
@@ -108,16 +110,32 @@
             device_id={"ri": to}, device_id_type=MESH,
         )
 
-    def start1(k, c):
-        swap(send1, recv1, s1, r1, k).start()
+    def nth(n):
+        turn, rest = lax.div(n, SHARE), lax.rem(n, SHARE)
+        dx, dz = lax.div(rest, ZT), lax.rem(rest, ZT)
+        return lax.rem(x + dx, NX) * NZ + lax.rem(lax.div(z, TURNS) + dz, ZT) * TURNS + turn
+
+    def swap1(to):
+        return pltpu.make_async_remote_copy(
+            src_ref=send1.at[to], dst_ref=recv1.at[me], send_sem=s1.at[to], recv_sem=r1.at[me],
+            device_id={"pair": to}, device_id_type=MESH,
+        )
+
+    def start1(n, c):
+        to = nth(n)
+
+        @pl.when(to != me)
+        def _():
+            swap1(to).start()
+
         return c
 
     g_up = along(dm, dall.at[ri], 0, up)
     g_down = along(dm, dall.at[ri], 1, down)
     g_sib = along(dm, dall.at[ri], 2, sib)
+    lax.fori_loop(0, GROUPS, start1, 0)
     g_up.start()
     g_down.start()
-    lax.fori_loop(1, GROUPS, start1, 0)
     g_sib.start()
     own1 = pltpu.make_async_copy(send1.at[me], recv1.at[me], local.at[0])
     own1.start()
@@ -149,7 +167,11 @@
     own1.wait()
 
     def end1(k, c):
-        swapped(send1, recv1, s1, r1, k).wait()
+        fro = lax.rem(me + k, GROUPS)
+        pltpu.make_async_remote_copy(
+            src_ref=send1.at[fro], dst_ref=recv1.at[fro], send_sem=s1.at[fro],
+            recv_sem=r1.at[fro], device_id={"pair": fro}, device_id_type=MESH,
+        ).wait()
         return c
 
     lax.fori_loop(1, GROUPS, end1, 0)
@@ -196,7 +218,7 @@
     lax.fori_loop(0, 8, third, 0)
 
     def pack(p):
-        l, t = pb[2 * p], pb[2 * p + 1]
+        l, t = pb[0, p], pb[1, p]
         tp, odd = lax.div(t, 2), lax.rem(t, 2)
         cols = []
         for a in range(8):
@@ -204,14 +226,25 @@
             cols.append(jnp.where(odd == 1, w[:24, 64:112], w[:24, 0:48]))
         send2[p] = jnp.concatenate(cols, axis=1)
 
+    def slot(pair):
+        w = lax.rem(pair, NZ)
+        return lax.rem(w, TURNS) * SHARE + lax.div(pair, NZ) * ZT + lax.div(w, TURNS)
+
+    def swap2(to):
+        return pltpu.make_async_remote_copy(
+            src_ref=send2.at[to], dst_ref=recv2.at[slot(me)], send_sem=s2.at[to],
+            recv_sem=r2.at[slot(me)], device_id={"pair": to}, device_id_type=MESH,
+        )
+
     def start2(k, c):
-        pack(lax.rem(me + k, GROUPS))
-        swap(send2, recv2, s2, r2, k).start()
+        to = lax.rem(me + k, GROUPS)
+        pack(to)
+        swap2(to).start()
         return c
 
     lax.fori_loop(1, GROUPS, start2, 0)
     pack(me)
-    own2 = pltpu.make_async_copy(send2.at[me], recv2.at[me], local.at[2])
+    own2 = pltpu.make_async_copy(send2.at[me], recv2.at[slot(me)], local.at[2])
     own2.start()
 
     along(dm.at[half], dall.at[far, half], 3, up).wait_recv()
@@ -223,105 +256,118 @@
     f_down.wait_recv()
     f_up.wait_recv()
     f_far.wait_recv()
-    own2.wait()
-
-    def end2(k, c):
-        swapped(send2, recv2, s2, r2, k).wait()
-        return c
-
-    lax.fori_loop(1, GROUPS, end2, 0)
-
-    for g in range(8):
-        v = nn(pc[...], recv2[g * 8 : (g + 1) * 8].reshape(192, 384)).astype(BF)
-        for mh in range(6):
-            img[g * 32 : (g + 1) * 32, mh * 384 : (mh + 1) * 384] = v[mh * 32 : (mh + 1) * 32]
 
     def part(xt):
         return jnp.concatenate([nt(img[...], dall[2 * xt]), nt(img[...], dall[2 * xt + 1])], axis=1)
 
-    def across(k):
+    def across(turn, k):
         return pltpu.make_async_remote_copy(
-            src_ref=xsend.at[k], dst_ref=xrecv.at[k], send_sem=sx.at[k], recv_sem=rx.at[k],
-            device_id={"pair": lax.rem(x + k + 1, NX) * NZ + z}, device_id_type=MESH,
-        )
-
-    for k in (1, 0, 2):
-        xsend[k] = part(lax.rem(x + k + 1, NX)).astype(BF)
-        across(k).start()
-    total = part(x)
-    for k in (1, 0, 2):
-        across(k).wait()
-        total = total + xrecv[k].astype(F32)
-    total = total.astype(BF)
-    for h in range(2):
-        for q in range(8):
-            zsend[q, h] = total[q * 32 : (q + 1) * 32, h * 256 : (h + 1) * 256]
-
-    def deal(q, h):
+            src_ref=xsend.at[turn, k], dst_ref=xrecv.at[turn, k], send_sem=sx.at[turn, k],
+            recv_sem=rx.at[turn, k], device_id={"pair": lax.rem(x + k + 1, NX) * NZ + z},
+            device_id_type=MESH,
+        )
+
+    def deal(turn, q, h):
         return pltpu.make_async_remote_copy(
-            src_ref=zsend.at[q, h], dst_ref=zrecv.at[z], send_sem=sz.at[q, h], recv_sem=rz.at[z],
+            src_ref=zsend.at[turn, q, h], dst_ref=zrecv.at[turn, z], send_sem=sz.at[turn, q, h],
+            recv_sem=rz.at[turn, z],
             device_id={"pair": x * NZ + core * 8 + q, "ri": y * 2 + h}, device_id_type=MESH,
-        )
-
-    def dealt(fro):
-        return pltpu.make_async_remote_copy(
-            src_ref=zsend.at[0, 0], dst_ref=zrecv.at[fro], send_sem=sz.at[0, 0],
-            recv_sem=rz.at[fro], device_id={"pair": x * NZ + fro, "ri": ri}, device_id_type=MESH,
         )
 
     mine = lax.div(z, 8) == core
     zq = lax.rem(z, 8)
-    for step in range(8):
-        q = lax.rem(zq + step, 8)
+
+    def kept(turn):
+        return pltpu.make_async_copy(zsend.at[turn, zq, core], zrecv.at[turn, z], local.at[3 + turn])
+
+    def each(turn, do):
+        for step in range(8):
+            q = lax.rem(zq + step, 8)
+            for h in range(2):
+                if step == 0:
+
+                    @pl.when(jnp.logical_not(mine & (core == h)))
+                    def _():
+                        do(deal(turn, q, h))
+                else:
+                    do(deal(turn, q, h))
+
+    for turn in range(TURNS):
+
+        @pl.when(lax.rem(z, TURNS) == turn)
+        def _():
+            own2.wait()
+
+        def arrive(n, c):
+            at = turn * SHARE + n
+
+            @pl.when(at != slot(me))
+            def _():
+                pltpu.make_async_remote_copy(
+                    src_ref=send2.at[0], dst_ref=recv2.at[at], send_sem=s2.at[0],
+                    recv_sem=r2.at[at], device_id={"pair": me}, device_id_type=MESH,
+                ).wait_recv()
+
+            return c
+
+        lax.fori_loop(0, SHARE, arrive, 0)
+        for g in range(SHARE // 8):
+            at = turn * SHARE + g * 8
+            v = nn(pc[...], recv2[at : at + 8].reshape(192, 384)).astype(BF)
+            for mh in range(6):
+                img[g * 32 : (g + 1) * 32, mh * 384 : (mh + 1) * 384] = v[mh * 32 : (mh + 1) * 32]
+        for k in (1, 0, 2):
+            xsend[turn, k] = part(lax.rem(x + k + 1, NX)).astype(BF)
+            across(turn, k).start()
+        total = part(x)
+        for k in (1, 0, 2):
+            across(turn, k).wait()
+            total = total + xrecv[turn, k].astype(F32)
+        total = total.astype(BF)
         for h in range(2):
-            if step == 0:
-                same = mine & (core == h)
-
-                @pl.when(same)
-                def _():
-                    pltpu.make_async_copy(zsend.at[q, h], zrecv.at[z], local.at[3]).start()
-
-                @pl.when(jnp.logical_not(same))
-                def _():
-                    deal(q, h).start()
-            else:
-                deal(q, h).start()
-    for step in range(8):
-        q = lax.rem(zq + step, 8)
-        for h in range(2):
-            if step == 0:
-                same = mine & (core == h)
-
-                @pl.when(jnp.logical_not(same))
-                def _():
-                    deal(q, h).wait_send()
-            else:
-                deal(q, h).wait_send()
-
-    @pl.when(mine)
-    def _():
-        pltpu.make_async_copy(zsend.at[0, 0], zrecv.at[z], local.at[3]).wait()
-
-    @pl.when(jnp.logical_not(mine))
-    def _():
-        dealt(z).wait_recv()
-
-    def end3(k, c):
-        dealt(lax.rem(z + k, NZ)).wait_recv()
-        return c
-
-    lax.fori_loop(1, NZ, end3, 0)
-    result = zrecv[0].astype(F32)
-    for k in range(1, NZ):
-        result = result + zrecv[k].astype(F32)
+            for q in range(8):
+                zsend[turn, q, h] = total[q * ZROWS : (q + 1) * ZROWS, h * 256 : (h + 1) * 256]
+        each(turn, lambda copy: copy.start())
+
+        @pl.when(mine)
+        def _():
+            kept(turn).start()
+
+    for turn in range(TURNS):
+        each(turn, lambda copy: copy.wait_send())
+
+        def dealt(fro):
+            return pltpu.make_async_remote_copy(
+                src_ref=zsend.at[0, 0, 0], dst_ref=zrecv.at[turn, fro], send_sem=sz.at[0, 0, 0],
+                recv_sem=rz.at[turn, fro], device_id={"pair": me}, device_id_type=MESH,
+            )
+
+        @pl.when(mine)
+        def _():
+            kept(turn).wait()
+
+        @pl.when(jnp.logical_not(mine))
+        def _():
+            dealt(z).wait_recv()
+
+        def end3(k, c):
+            dealt(lax.rem(z + k, NZ)).wait_recv()
+            return c
+
+        lax.fori_loop(1, NZ, end3, 0)
+        some = zrecv[turn, 0].astype(F32)
+        for k in range(1, NZ):
+            some = some + zrecv[turn, k].astype(F32)
+        for j in range(8 // TURNS):
+            at = (j * TURNS + turn) * 4
+            fsend[at : at + 4] = some[j * 4 : j * 4 + 4]
 
     @pl.when(x == y)
     def _():
-        out[...] = result
+        out[...] = fsend[...]
 
     @pl.when(x != y)
     def _():
-        fsend[...] = result
         turn = pltpu.make_async_remote_copy(
             src_ref=fsend, dst_ref=out, send_sem=sf, recv_sem=rf,
             device_id={"pair": y * NZ + z, "ri": x * 2 + core}, device_id_type=MESH,
@@ -329,6 +375,11 @@
         turn.start()
         turn.wait()
 
+    def sent2(k, c):
+        swap2(lax.rem(me + k, GROUPS)).wait_send()
+        return c
+
+    lax.fori_loop(1, GROUPS, sent2, 0)
     g_up.wait_send()
     g_down.wait_send()
     g_sib.wait_send()
@@ -340,8 +391,6 @@
 
 
 def on_device(tensor, pattern, pair_blocks, green_occ, green_virt):
-    mask = jnp.repeat(pattern, RB, axis=1).astype(tensor.dtype)
-    masked = (tensor * mask[:, :, None])[0]
     index = pair_blocks[:, 0] * NB + pair_blocks[:, 1]
     hits = index[None, :] == jnp.arange(NB * NB, dtype=jnp.int32)[:, None]
     order = jnp.arange(GROUPS, dtype=jnp.int32)[None, :]
@@ -352,9 +401,11 @@
     chi = pl.pallas_call(
         kernel,
         out_shape=jax.ShapeDtypeStruct((32, 256), F32),
-        in_specs=[smem, smem, vmem, vmem, vmem, vmem],
+        in_specs=[smem, smem, smem, vmem, vmem, vmem],
         out_specs=vmem,
         scratch_shapes=[
+            pltpu.VMEM((GROUPS, 24, 384), BF),
+            pltpu.VMEM((256, BB), BF),
             pltpu.VMEM((GROUPS + 1, 24, 384), BF),
             pltpu.VMEM((8, 256, BB), BF),
             pltpu.VMEM((8, 6, 12, 32, 128), BF),
@@ -363,11 +414,11 @@
             pltpu.VMEM((8, 6, 12, 32, 128), BF),
             pltpu.VMEM((GROUPS, 24, 384), BF),
             pltpu.VMEM((GROUPS, 24, 384), BF),
-            pltpu.VMEM((256, BB), BF),
-            pltpu.VMEM((3, 256, 512), BF),
-            pltpu.VMEM((3, 256, 512), BF),
-            pltpu.VMEM((8, 2, 32, 256), BF),
-            pltpu.VMEM((NZ, 32, 256), BF),
+            pltpu.VMEM((SHARE * 4, BB), BF),
+            pltpu.VMEM((TURNS, 3, SHARE * 4, 512), BF),
+            pltpu.VMEM((TURNS, 3, SHARE * 4, 512), BF),
+            pltpu.VMEM((TURNS, 8, 2, ZROWS, 256), BF),
+            pltpu.VMEM((TURNS, NZ, ZROWS, 256), BF),
             pltpu.VMEM((32, 256), F32),
             pltpu.VMEM((768, 768), BF),
             pltpu.VMEM((640, 640), BF),
@@ -377,15 +428,15 @@
             dma((GROUPS,)), dma((GROUPS,)),
             dma((8,)), dma((8,)),
             dma((GROUPS,)), dma((GROUPS,)),
-            dma((3,)), dma((3,)),
-            dma((8, 2)), dma((NZ,)),
+            dma((TURNS, 3)), dma((TURNS, 3)),
+            dma((TURNS, 8, 2)), dma((TURNS, NZ)),
             dma, dma,
-            dma((4,)),
+            dma((3 + TURNS,)),
         ],
         compiler_params=pltpu.CompilerParams(
             collective_id=0, has_side_effects=True, vmem_limit_bytes=60 << 20
         ),
-    )(inverse, pair_blocks.reshape(-1), masked.reshape(GROUPS, 24, 384), masked, green_virt, green_occ)
+    )(inverse, pair_blocks.T, pattern, tensor, green_virt, green_occ)
     return chi.T
 
 

time: 194 us -> 176 us (0.907)
  Pallas kernels: 184 us -> 172 us
  local copies, waits for them, and re-layouts: 4.21 us -> 1.38 us
  other arithmetic: 3.93 us -> 1.41 us
    pallas_call x1, Pallas kernels: 184 us -> 172 us  [on_device(): pl.pallas_call(kernel, out_shape=jax.ShapeDtypeStruct((32, 256), F32), in...]
where the time goes in v2:
time: 176 us; the launch traced here: 175 us
  Pallas kernels  172 us (98%)
    pallas_call x1, Pallas kernels, on_device(): pl.pallas_call(kernel, out_shape=jax.ShapeDtypeStruct((32, 256), F32), in...  172 us

profile of v2, /device:TPU:7, one launch (start us, length us, event | category | flops | bytes accessed | tf_op | source)
XLA Modules:
  0.0 175.2 jit_solution(11122472671334237202)
XLA Ops:
  0.0 0.8 add_bitcast_fusion
  0.8 0.7 select_reduce_fusion.inv
  1.4 172.4 %shard_map.55 = f32[32,256]{1,0:T(8,128)} custom-call(s32[144]{0:T(256)} %select_reduce_fusion.inv, s32[2,64]{1,0:T(2,128)} %bitcast.5, s32[1,8]{1,0:T(1,128)} %pattern.1, bf16[1,256,2304]{2,1,0:T(8,128)(2,1)} %tensor.1, bf16[576,576]{1,0:T(8,128)(2,1)} %gv.1, bf16[576,576]{1,0:T(8,128)(2,1)} %go.1), custom_call_target="tpu_custom_call" | custom-call | tf_op jit(solution)/shard_map/pallas_call | solution.py:401
  173.8 1.4 copy.7

commit v3 on v2

--- a/solution.py
+++ b/solution.py
@@ -38,32 +38,37 @@
     return (u == BLK * lax.div(r, 64) + lax.rem(r, 64)) & (lax.rem(r, 64) < BLK)
 
 
-def pad80(r, u):
-    return (u == 8 * lax.rem(r, 80) + lax.div(r, 80)) & (lax.rem(r, 80) < 72)
-
-
-def by_q(r, c):
-    q, w = lax.div(r, 80), lax.rem(r, 80)
-    return (c == lax.div(w, 6) * 32 + q * 6 + lax.rem(w, 6)) & (w < 72)
-
-
-def by_block(r, c):
-    return by_q(c, r)
-
-
-def from_m(r, c):
-    return by_m(c, r)
-
-
-def by_m(r, c):
-    mh, rest = lax.div(r, 32), lax.rem(r, 32)
-    return c == rest * 6 + mh
+def pad32(r, u):
+    b, w = lax.div(r, 384), lax.rem(r, 384)
+    return (u == BLK * lax.div(w, 32) + 2 * lax.rem(w, 32) + b) & (lax.rem(w, 32) < 24)
+
+
+def to_slab(r, c):
+    d, w = lax.div(c, 192), lax.rem(c, 192)
+    q = lax.rem(w, 4)
+    at = lax.div(lax.rem(w, 32), 4) * 24 + lax.div(w, 32) * 4
+    return r == at + lax.rem(q + 4 - d, 4)
+
+
+def from_slab(r, c):
+    d, w = lax.div(c, 192), lax.rem(c, 192)
+    g, mh, rr = lax.div(w, 24), lax.div(lax.rem(w, 24), 4), lax.rem(w, 4)
+    return r == mh * 32 + g * 4 + lax.rem(rr + d, 4)
+
+
+def shifted(v, sign):
+    row = lax.broadcasted_iota(jnp.int32, v.shape, 0)
+    lane = lax.broadcasted_iota(jnp.int32, v.shape, 1)
+    keep = lax.rem(row, 4) == lax.div(lane, 96)
+    zero = jnp.zeros_like(v)
+    rolled = [v] + [pltpu.roll(v, (sign * 96 * d) % 384, 1) for d in (1, 2, 3)]
+    return jnp.concatenate([jnp.where(keep, u, zero) for u in rolled], axis=0)
 
 
 def kernel(
     inv, pb, pattern, tensor, gv, go, out,
-    send1, dm, recv1, dall, dense, xs, ys, ws, send2, recv2, img, xsend, xrecv, zsend, zrecv, fsend,
-    gvp, gop, pa, pbk, pc,
+    send1, dm, recv1, dall, dense, ws, send2, recv2, img, xsend, xrecv, zsend, zrecv, fsend,
+    gvp, gop, pc,
     s1, r1, sy, ry, s2, r2, sx, rx, sz, rz, sf, rf, local,
 ):
     me = lax.axis_index("pair")
@@ -94,13 +99,13 @@
     def _():
         greet(y * NZ + z, x * 2 + core)
 
-    pc[...] = one_hot(192, 192, from_m)
+    pc[...] = one_hot(192, 768, to_slab)
     for g in range(8):
         rows = slice(g * RB, (g + 1) * RB)
         masked = tensor[0, rows] * pattern[0, g].astype(BF)
         dm[rows] = masked
         v = jnp.concatenate([masked[:, m * 384 : (m + 1) * 384] for m in range(6)], axis=0)
-        send1[g * 8 : (g + 1) * 8] = nn(pc[...], v).astype(BF).reshape(8, 24, 384)
+        send1[g * 8 : (g + 1) * 8] = nn(pc[...], shifted(v, 1)).astype(BF).reshape(8, 24, 384)
 
     pl.semaphore_wait(bar, GROUPS - 1 + NZ + 2 + jnp.where(x != y, 1, 0))
 
@@ -145,11 +150,9 @@
 
     e = one_hot(768, 576, pad64)
     gvp[...] = nt(nt(e, gv[...]).astype(BF), e).astype(BF)
-    f = one_hot(640, 576, pad80)
+    f = one_hot(768, 576, pad32)
     gop[...] = nt(nn(f, go[...]).astype(BF), f).astype(BF)
-    pa[...] = one_hot(320, 384, by_q)
-    pbk[...] = one_hot(384, 320, by_block)
-    pc[...] = one_hot(192, 192, by_m)
+    pc[...] = one_hot(192, 768, from_slab)
 
     half = pl.ds(0, 128)
     rest = pl.ds(128, 128)
@@ -176,55 +179,61 @@
 
     lax.fori_loop(1, GROUPS, end1, 0)
 
+    lane = lax.broadcasted_iota(jnp.int32, (32, 128), 1)
+
+    def cut(tiles, n, at):
+        t, low = n * BLK // 128, n * BLK % 128
+        piece = pltpu.roll(tiles[t], (at - low) % 128, 1)
+        if low + BLK > 128:
+            more = pltpu.roll(tiles[t + 1], (at - low) % 128, 1)
+            piece = jnp.where(lane < at + 128 - low, piece, more)
+        return piece
+
     def place(n, c):
         i, jp = lax.div(n, 6), lax.rem(n, 6)
-        lowr = jnp.zeros((8, 384), BF)
-        b0 = jnp.concatenate([recv1[inv[2 * n]], lowr], axis=0)
-        b1 = jnp.concatenate([recv1[inv[2 * n + 1]], lowr], axis=0)
-        gap = jnp.zeros((32, 16), BF)
         low = jnp.zeros((8, 128), BF)
+
+        def tiles(p):
+            return [
+                jnp.concatenate([recv1[p, :, t * 128 : (t + 1) * 128], low], axis=0)
+                for t in range(3)
+            ]
+
+        b0, b1 = tiles(inv[2 * n]), tiles(inv[2 * n + 1])
         for a in range(8):
-            cut = slice(a * BLK, (a + 1) * BLK)
-            row = jnp.concatenate([b0[:, cut], gap, b1[:, cut], gap], axis=1)
-            dense[a, jp, i] = row
+            dense[a // 2, jp, a % 2, i] = jnp.where(lane < 64, cut(b0, a, 0), cut(b1, a, 64))
         return c
 
     lax.fori_loop(0, 72, place, 0)
 
-    def first(a, c):
-        d = jnp.concatenate([dense[a, jp].reshape(384, 128) for jp in range(6)], axis=1)
-        d = nn(pa[...], d).astype(BF)
+    def image(q, c):
+        d = jnp.concatenate([dense[q, jp].reshape(768, 128) for jp in range(6)], axis=1)
         h = nn(d, gvp[...]).astype(BF)
-        for q in range(4):
-            xs[q, a] = h[q * 80 : (q + 1) * 80]
-        return c
-
-    lax.fori_loop(0, 8, first, 0)
-
-    def second(q, c):
-        v = nn(gop[...], xs[q].reshape(640, 768)).astype(BF)
-        for a in range(8):
-            ys[a, q] = v[a * 80 : (a + 1) * 80]
-        return c
-
-    lax.fori_loop(0, 4, second, 0)
-
-    def third(a, c):
-        v = nn(pbk[...], ys[a].reshape(320, 768)).astype(BF)
+        v = nn(gop[...], h).astype(BF)
         for tp in range(6):
-            ws[a, tp] = v[:, tp * 128 : (tp + 1) * 128].reshape(12, 32, 128)
-        return c
-
-    lax.fori_loop(0, 8, third, 0)
+            ws[q, tp] = v[:, tp * 128 : (tp + 1) * 128].reshape(2, 12, 32, 128)
+        return c
+
+    lax.fori_loop(0, 4, image, 0)
 
     def pack(p):
         l, t = pb[0, p], pb[1, p]
         tp, odd = lax.div(t, 2), lax.rem(t, 2)
-        cols = []
+        rolled = []
         for a in range(8):
-            w = ws[a, tp, l]
-            cols.append(jnp.where(odd == 1, w[:24, 64:112], w[:24, 0:48]))
-        send2[p] = jnp.concatenate(cols, axis=1)
+            w = ws[a // 2, tp, a % 2, l]
+            at = a * BLK % 128
+            rolled.append(jnp.where(odd == 1, pltpu.roll(w, (at + 64) % 128, 1), pltpu.roll(w, at, 1)))
+        for t in range(3):
+            out_tile = None
+            for a in reversed(range(8)):
+                first, last = a * BLK - t * 128, (a + 1) * BLK - t * 128
+                if last > 0 and first < 128:
+                    if out_tile is None:
+                        out_tile = rolled[a]
+                    else:
+                        out_tile = jnp.where(lane < last, rolled[a], out_tile)
+            send2[p, :, t * 128 : (t + 1) * 128] = out_tile[:24]
 
     def slot(pair):
         w = lax.rem(pair, NZ)
@@ -313,7 +322,7 @@
         lax.fori_loop(0, SHARE, arrive, 0)
         for g in range(SHARE // 8):
             at = turn * SHARE + g * 8
-            v = nn(pc[...], recv2[at : at + 8].reshape(192, 384)).astype(BF)
+            v = nn(pc[...], shifted(recv2[at : at + 8].reshape(192, 384), -1)).astype(BF)
             for mh in range(6):
                 img[g * 32 : (g + 1) * 32, mh * 384 : (mh + 1) * 384] = v[mh * 32 : (mh + 1) * 32]
         for k in (1, 0, 2):
@@ -408,10 +417,8 @@
             pltpu.VMEM((256, BB), BF),
             pltpu.VMEM((GROUPS + 1, 24, 384), BF),
             pltpu.VMEM((8, 256, BB), BF),
-            pltpu.VMEM((8, 6, 12, 32, 128), BF),
-            pltpu.VMEM((4, 8, 80, 768), BF),
-            pltpu.VMEM((8, 4, 80, 768), BF),
-            pltpu.VMEM((8, 6, 12, 32, 128), BF),
+            pltpu.VMEM((4, 6, 2, 12, 32, 128), BF),
+            pltpu.VMEM((4, 6, 2, 12, 32, 128), BF),
             pltpu.VMEM((GROUPS, 24, 384), BF),
             pltpu.VMEM((GROUPS, 24, 384), BF),
             pltpu.VMEM((SHARE * 4, BB), BF),
@@ -421,10 +428,8 @@
             pltpu.VMEM((TURNS, NZ, ZROWS, 256), BF),
             pltpu.VMEM((32, 256), F32),
             pltpu.VMEM((768, 768), BF),
-            pltpu.VMEM((640, 640), BF),
-            pltpu.VMEM((320, 384), BF),
-            pltpu.VMEM((384, 320), BF),
-            pltpu.VMEM((192, 192), BF),
+            pltpu.VMEM((768, 768), BF),
+            pltpu.VMEM((192, 768), BF),
             dma((GROUPS,)), dma((GROUPS,)),
             dma((8,)), dma((8,)),
             dma((GROUPS,)), dma((GROUPS,)),

time: 176 us -> 169 us (0.960)
  Pallas kernels: 172 us -> 165 us
    pallas_call x1, Pallas kernels: 172 us -> 165 us  [on_device(): pl.pallas_call(kernel, out_shape=jax.ShapeDtypeStruct((32, 256), F32), in...]
where the time goes in v3:
time: 169 us; the launch traced here: 168 us
  Pallas kernels  165 us (98%)
    pallas_call x1, Pallas kernels, on_device(): pl.pallas_call(kernel, out_shape=jax.ShapeDtypeStruct((32, 256), F32), in...  165 us

profile of v3, /device:TPU:7, one launch (start us, length us, event | category | flops | bytes accessed | tf_op | source)
XLA Modules:
  0.0 168.0 jit_solution(17945326072774703786)
XLA Ops:
  0.0 0.8 add_bitcast_fusion
  0.8 0.7 select_reduce_fusion.inv
  1.4 165.2 %shard_map.55 = f32[32,256]{1,0:T(8,128)} custom-call(s32[144]{0:T(256)} %select_reduce_fusion.inv, s32[2,64]{1,0:T(2,128)} %bitcast.5, s32[1,8]{1,0:T(1,128)} %pattern.1, bf16[1,256,2304]{2,1,0:T(8,128)(2,1)} %tensor.1, bf16[576,576]{1,0:T(8,128)(2,1)} %gv.1, bf16[576,576]{1,0:T(8,128)(2,1)} %go.1), custom_call_target="tpu_custom_call" | custom-call | tf_op jit(solution)/shard_map/pallas_call | solution.py:410
  166.6 1.4 copy.7

commit v4 on v3

--- a/solution.py
+++ b/solution.py
@@ -66,9 +66,9 @@
 
 
 def kernel(
-    inv, pb, pattern, tensor, gv, go, out,
-    send1, dm, recv1, dall, dense, ws, send2, recv2, img, xsend, xrecv, zsend, zrecv, fsend,
-    gvp, gop, pc,
+    pb, pb_rows, pattern, tensor, gv, go, out,
+    send1, dm, recv1, dall, dense, ws, send2, recv2, img, held, xsend, xrecv, zsend, zrecv, fsend,
+    gvp, gop, pc, holder, inv,
     s1, r1, sy, ry, s2, r2, sx, rx, sz, rz, sf, rf, local,
 ):
     me = lax.axis_index("pair")
@@ -99,13 +99,27 @@
     def _():
         greet(y * NZ + z, x * 2 + core)
 
+    pairs = lax.broadcasted_iota(jnp.int32, (GROUPS, GROUPS), 0)
+    same = pairs == lax.broadcasted_iota(jnp.int32, (GROUPS, GROUPS), 1)
+    index = pb_rows[0:1] * NB + pb_rows[1:2]
+    index = jnp.sum(jnp.where(same, index, 0), axis=1, keepdims=True)
+    hits = index == lax.broadcasted_iota(jnp.int32, (GROUPS, 256), 1)
+    order = lax.broadcasted_iota(jnp.int32, (GROUPS, 256), 0)
+    holder[...] = jnp.broadcast_to(jnp.min(jnp.where(hits, order, GROUPS), axis=0, keepdims=True), (8, 256))
+    to_smem = pltpu.make_async_copy(holder, inv, local.at[3])
+    to_smem.start()
+
     pc[...] = one_hot(192, 768, to_slab)
-    for g in range(8):
-        rows = slice(g * RB, (g + 1) * RB)
+
+    def mask(g, c):
+        rows = pl.ds(pl.multiple_of(g * RB, RB), RB)
         masked = tensor[0, rows] * pattern[0, g].astype(BF)
         dm[rows] = masked
         v = jnp.concatenate([masked[:, m * 384 : (m + 1) * 384] for m in range(6)], axis=0)
-        send1[g * 8 : (g + 1) * 8] = nn(pc[...], shifted(v, 1)).astype(BF).reshape(8, 24, 384)
+        send1[pl.ds(g * 8, 8)] = nn(pc[...], shifted(v, 1)).astype(BF).reshape(8, 24, 384)
+        return c
+
+    lax.fori_loop(0, 8, mask, 0)
 
     pl.semaphore_wait(bar, GROUPS - 1 + NZ + 2 + jnp.where(x != y, 1, 0))
 
@@ -168,6 +182,7 @@
     f_up.start()
 
     own1.wait()
+    to_smem.wait()
 
     def end1(k, c):
         fro = lax.rem(me + k, GROUPS)
@@ -199,12 +214,12 @@
                 for t in range(3)
             ]
 
-        b0, b1 = tiles(inv[2 * n]), tiles(inv[2 * n + 1])
+        b0, b1 = tiles(inv[0, 2 * n]), tiles(inv[0, 2 * n + 1])
         for a in range(8):
             dense[a // 2, jp, a % 2, i] = jnp.where(lane < 64, cut(b0, a, 0), cut(b1, a, 64))
         return c
 
-    lax.fori_loop(0, 72, place, 0)
+    lax.fori_loop(0, 72, place, 0, unroll=4)
 
     def image(q, c):
         d = jnp.concatenate([dense[q, jp].reshape(768, 128) for jp in range(6)], axis=1)
@@ -251,7 +266,7 @@
         swap2(to).start()
         return c
 
-    lax.fori_loop(1, GROUPS, start2, 0)
+    lax.fori_loop(1, GROUPS, start2, 0, unroll=3)
     pack(me)
     own2 = pltpu.make_async_copy(send2.at[me], recv2.at[slot(me)], local.at[2])
     own2.start()
@@ -266,14 +281,11 @@
     f_up.wait_recv()
     f_far.wait_recv()
 
-    def part(xt):
-        return jnp.concatenate([nt(img[...], dall[2 * xt]), nt(img[...], dall[2 * xt + 1])], axis=1)
-
-    def across(turn, k):
+    def across(turn, k, h):
         return pltpu.make_async_remote_copy(
-            src_ref=xsend.at[turn, k], dst_ref=xrecv.at[turn, k], send_sem=sx.at[turn, k],
-            recv_sem=rx.at[turn, k], device_id={"pair": lax.rem(x + k + 1, NX) * NZ + z},
-            device_id_type=MESH,
+            src_ref=xsend.at[turn, k, h], dst_ref=xrecv.at[turn, k, h],
+            send_sem=sx.at[turn, k, h], recv_sem=rx.at[turn, k, h],
+            device_id={"pair": lax.rem(x + k + 1, NX) * NZ + z}, device_id_type=MESH,
         )
 
     def deal(turn, q, h):
@@ -289,19 +301,33 @@
     def kept(turn):
         return pltpu.make_async_copy(zsend.at[turn, zq, core], zrecv.at[turn, z], local.at[3 + turn])
 
-    def each(turn, do):
-        for step in range(8):
-            q = lax.rem(zq + step, 8)
-            for h in range(2):
-                if step == 0:
-
-                    @pl.when(jnp.logical_not(mine & (core == h)))
-                    def _():
-                        do(deal(turn, q, h))
-                else:
-                    do(deal(turn, q, h))
-
-    for turn in range(TURNS):
+    def each(turn, h, do):
+        def one(step, c):
+            @pl.when(jnp.logical_not((step == 0) & mine & (core == h)))
+            def _():
+                do(deal(turn, lax.rem(zq + step, 8), h))
+
+            return c
+
+        lax.fori_loop(0, 8, one, 0)
+
+    g_up.wait_send()
+    g_down.wait_send()
+    g_sib.wait_send()
+    h_up.wait_send()
+    h_down.wait_send()
+    f_down.wait_send()
+    f_up.wait_send()
+
+    def sent2(k, c):
+        swap2(lax.rem(me + k, GROUPS)).wait_send()
+        return c
+
+    def add_up(turn, c):
+        @pl.when(turn == TURNS - 1)
+        def _():
+            lax.fori_loop(1, GROUPS, sent2, 0)
+            f_far.wait_send()
 
         @pl.when(lax.rem(z, TURNS) == turn)
         def _():
@@ -320,30 +346,54 @@
             return c
 
         lax.fori_loop(0, SHARE, arrive, 0)
-        for g in range(SHARE // 8):
-            at = turn * SHARE + g * 8
-            v = nn(pc[...], shifted(recv2[at : at + 8].reshape(192, 384), -1)).astype(BF)
+        def gather(g, c):
+            v = shifted(recv2[pl.ds(turn * SHARE + g * 8, 8)].reshape(192, 384), -1)
+            v = nn(pc[...], v).astype(BF)
+            rows = pl.ds(pl.multiple_of(g * 32, 32), 32)
             for mh in range(6):
-                img[g * 32 : (g + 1) * 32, mh * 384 : (mh + 1) * 384] = v[mh * 32 : (mh + 1) * 32]
-        for k in (1, 0, 2):
-            xsend[turn, k] = part(lax.rem(x + k + 1, NX)).astype(BF)
-            across(turn, k).start()
-        total = part(x)
-        for k in (1, 0, 2):
-            across(turn, k).wait()
-            total = total + xrecv[turn, k].astype(F32)
-        total = total.astype(BF)
-        for h in range(2):
+                img[rows, mh * 384 : (mh + 1) * 384] = v[mh * 32 : (mh + 1) * 32]
+            return c
+
+        lax.fori_loop(0, SHARE // 8, gather, 0)
+
+        def part(n, c):
+            step, h = lax.div(n, 2), lax.rem(n, 2)
+            far_x = lax.rem(lax.rem(step + 1, 3) + 1, 4)
+            to_x = jnp.where(step == 3, 0, far_x)
+            held[h] = nt(img[...], dall[2 * lax.rem(x + to_x, NX) + h])
+
+            @pl.when(step < 3)
+            def _():
+                k = lax.rem(step + 1, 3)
+                xsend[turn, k, h] = held[h].astype(BF)
+                across(turn, k, h).start()
+
+            return c
+
+        lax.fori_loop(0, 8, part, 0)
+
+        def onward(h, c):
+            total = held[h]
+            for k in range(3):
+                across(turn, k, h).wait()
+                total = total + xrecv[turn, k, h].astype(F32)
+            total = total.astype(BF)
             for q in range(8):
-                zsend[turn, q, h] = total[q * ZROWS : (q + 1) * ZROWS, h * 256 : (h + 1) * 256]
-        each(turn, lambda copy: copy.start())
-
-        @pl.when(mine)
-        def _():
-            kept(turn).start()
+                zsend[turn, q, h] = total[q * ZROWS : (q + 1) * ZROWS]
+            each(turn, h, lambda copy: copy.start())
+
+            @pl.when(mine & (core == h))
+            def _():
+                kept(turn).start()
+
+            return c
+
+        lax.fori_loop(0, 2, onward, 0)
+        return c
+
+    lax.fori_loop(0, TURNS, add_up, 0)
 
     for turn in range(TURNS):
-        each(turn, lambda copy: copy.wait_send())
 
         def dealt(fro):
             return pltpu.make_async_remote_copy(
@@ -375,42 +425,32 @@
     def _():
         out[...] = fsend[...]
 
+    turned = pltpu.make_async_remote_copy(
+        src_ref=fsend, dst_ref=out, send_sem=sf, recv_sem=rf,
+        device_id={"pair": y * NZ + z, "ri": x * 2 + core}, device_id_type=MESH,
+    )
+
     @pl.when(x != y)
     def _():
-        turn = pltpu.make_async_remote_copy(
-            src_ref=fsend, dst_ref=out, send_sem=sf, recv_sem=rf,
-            device_id={"pair": y * NZ + z, "ri": x * 2 + core}, device_id_type=MESH,
-        )
-        turn.start()
-        turn.wait()
-
-    def sent2(k, c):
-        swap2(lax.rem(me + k, GROUPS)).wait_send()
-        return c
-
-    lax.fori_loop(1, GROUPS, sent2, 0)
-    g_up.wait_send()
-    g_down.wait_send()
-    g_sib.wait_send()
-    h_up.wait_send()
-    h_down.wait_send()
-    f_down.wait_send()
-    f_up.wait_send()
-    f_far.wait_send()
+        turned.start()
+
+    for turn in range(TURNS):
+        for h in range(2):
+            each(turn, h, lambda copy: copy.wait_send())
+
+    @pl.when(x != y)
+    def _():
+        turned.wait()
 
 
 def on_device(tensor, pattern, pair_blocks, green_occ, green_virt):
-    index = pair_blocks[:, 0] * NB + pair_blocks[:, 1]
-    hits = index[None, :] == jnp.arange(NB * NB, dtype=jnp.int32)[:, None]
-    order = jnp.arange(GROUPS, dtype=jnp.int32)[None, :]
-    inverse = jnp.min(jnp.where(hits, order, GROUPS), axis=1).astype(jnp.int32)
     vmem = pl.BlockSpec(memory_space=pltpu.VMEM)
     smem = pl.BlockSpec(memory_space=pltpu.SMEM)
     dma = pltpu.SemaphoreType.DMA
     chi = pl.pallas_call(
         kernel,
         out_shape=jax.ShapeDtypeStruct((32, 256), F32),
-        in_specs=[smem, smem, smem, vmem, vmem, vmem],
+        in_specs=[smem, vmem, smem, vmem, vmem, vmem],
         out_specs=vmem,
         scratch_shapes=[
             pltpu.VMEM((GROUPS, 24, 384), BF),
@@ -422,18 +462,21 @@
             pltpu.VMEM((GROUPS, 24, 384), BF),
             pltpu.VMEM((GROUPS, 24, 384), BF),
             pltpu.VMEM((SHARE * 4, BB), BF),
-            pltpu.VMEM((TURNS, 3, SHARE * 4, 512), BF),
-            pltpu.VMEM((TURNS, 3, SHARE * 4, 512), BF),
+            pltpu.VMEM((2, SHARE * 4, 256), F32),
+            pltpu.VMEM((TURNS, 3, 2, SHARE * 4, 256), BF),
+            pltpu.VMEM((TURNS, 3, 2, SHARE * 4, 256), BF),
             pltpu.VMEM((TURNS, 8, 2, ZROWS, 256), BF),
             pltpu.VMEM((TURNS, NZ, ZROWS, 256), BF),
             pltpu.VMEM((32, 256), F32),
             pltpu.VMEM((768, 768), BF),
             pltpu.VMEM((768, 768), BF),
             pltpu.VMEM((192, 768), BF),
+            pltpu.VMEM((8, 256), jnp.int32),
+            pltpu.SMEM((8, 256), jnp.int32),
             dma((GROUPS,)), dma((GROUPS,)),
             dma((8,)), dma((8,)),
             dma((GROUPS,)), dma((GROUPS,)),
-            dma((TURNS, 3)), dma((TURNS, 3)),
+            dma((TURNS, 3, 2)), dma((TURNS, 3, 2)),
             dma((TURNS, 8, 2)), dma((TURNS, NZ)),
             dma, dma,
             dma((3 + TURNS,)),
@@ -441,7 +484,7 @@
         compiler_params=pltpu.CompilerParams(
             collective_id=0, has_side_effects=True, vmem_limit_bytes=60 << 20
         ),
-    )(inverse, pair_blocks.T, pattern, tensor, green_virt, green_occ)
+    )(pair_blocks.T, pair_blocks.T, pattern, tensor, green_virt, green_occ)
     return chi.T
 
 

time: 169 us -> 164 us (0.970)
  Pallas kernels: 165 us -> 163 us
    pallas_call x1, Pallas kernels: 165 us -> 163 us  [on_device(): pl.pallas_call(kernel, out_shape=jax.ShapeDtypeStruct((32, 256), F32), in...]
where the time goes in v4:
time: 164 us
  Pallas kernels  163 us (99%)
    pallas_call x1, Pallas kernels, on_device(): pl.pallas_call(kernel, out_shape=jax.ShapeDtypeStruct((32, 256), F32), in...  163 us

profile of v4, /device:TPU:7, one launch (start us, length us, event | category | flops | bytes accessed | tf_op | source)
XLA Modules:
  0.0 164.2 jit_solution(10696087580036736449)
XLA Ops:
  0.0 162.8 %shard_map.55 = f32[32,256]{1,0:T(8,128)} custom-call(s32[2,64]{1,0:T(2,128)} %bitcast.3, s32[2,64]{1,0:T(2,128)} %bitcast.4, s32[1,8]{1,0:T(1,128)} %pattern.1, bf16[1,256,2304]{2,1,0:T(8,128)(2,1)} %tensor.1, bf16[576,576]{1,0:T(8,128)(2,1)} %gv.1, bf16[576,576]{1,0:T(8,128)(2,1)} %go.1), custom_call_target="tpu_custom_call" | custom-call | tf_op jit(solution)/shard_map/pallas_call | solution.py:450
  162.8 1.4 copy.7

commit v5 on v4

--- a/solution.py
+++ b/solution.py
@@ -219,7 +219,7 @@
             dense[a // 2, jp, a % 2, i] = jnp.where(lane < 64, cut(b0, a, 0), cut(b1, a, 64))
         return c
 
-    lax.fori_loop(0, 72, place, 0, unroll=4)
+    lax.fori_loop(0, 72, place, 0, unroll=8)
 
     def image(q, c):
         d = jnp.concatenate([dense[q, jp].reshape(768, 128) for jp in range(6)], axis=1)
@@ -266,7 +266,7 @@
         swap2(to).start()
         return c
 
-    lax.fori_loop(1, GROUPS, start2, 0, unroll=3)
+    lax.fori_loop(1, GROUPS, start2, 0, unroll=7)
     pack(me)
     own2 = pltpu.make_async_copy(send2.at[me], recv2.at[slot(me)], local.at[2])
     own2.start()
@@ -357,7 +357,7 @@
         lax.fori_loop(0, SHARE // 8, gather, 0)
 
         def part(n, c):
-            step, h = lax.div(n, 2), lax.rem(n, 2)
+            step, h = lax.rem(n, 4), lax.div(n, 4)
             far_x = lax.rem(lax.rem(step + 1, 3) + 1, 4)
             to_x = jnp.where(step == 3, 0, far_x)
             held[h] = nt(img[...], dall[2 * lax.rem(x + to_x, NX) + h])

time: 164 us -> 163 us (level)
  Pallas kernels: 163 us -> 161 us
    pallas_call x1, Pallas kernels: 163 us -> 161 us  [on_device(): pl.pallas_call(kernel, out_shape=jax.ShapeDtypeStruct((32, 256), F32), in...]
where the time goes in v5:
time: 163 us; the launch traced here: 162 us
  Pallas kernels  161 us (99%)
    pallas_call x1, Pallas kernels, on_device(): pl.pallas_call(kernel, out_shape=jax.ShapeDtypeStruct((32, 256), F32), in...  161 us

profile of v5, /device:TPU:7, one launch (start us, length us, event | category | flops | bytes accessed | tf_op | source)
XLA Modules:
  0.0 162.5 jit_solution(4256238265263260636)
XLA Ops:
  0.0 161.1 %shard_map.55 = f32[32,256]{1,0:T(8,128)} custom-call(s32[2,64]{1,0:T(2,128)} %bitcast.3, s32[2,64]{1,0:T(2,128)} %bitcast.4, s32[1,8]{1,0:T(1,128)} %pattern.1, bf16[1,256,2304]{2,1,0:T(8,128)(2,1)} %tensor.1, bf16[576,576]{1,0:T(8,128)(2,1)} %gv.1, bf16[576,576]{1,0:T(8,128)(2,1)} %go.1), custom_call_target="tpu_custom_call" | custom-call | tf_op jit(solution)/shard_map/pallas_call | solution.py:450
  161.1 1.4 copy.7
